TPU v7x, 256 devices: a whole 4x4x8 slice. The times are simulated.
256 devices in a mesh: row: 16 (over x_lo, z), col: 16 (over x_hi, y, core).
Axes of the slice: x: 4 (x_hi: 2, x_lo: 2; x = x_hi * 2 + x_lo), y: 4, z: 8, core: 2. Of those that a mesh axis runs over, the one named last changes fastest.
Arguments:
- points: bfloat16 [96, 1024, 1024], P('row', 'col')
- targets: bfloat16 [96, 1024, 1000], P('row', 'col'), may hold values from -6 to 6
- coeffs: float32 [96, 1024, 1000], P('row', 'col'), may hold values from -0.25 to 0.25
- block_inverse: float32 [96, 1024, 1024], P('row', 'col')
- block_order: int32 [96], replicated, may hold values from 0 to 95, each once
Outputs:
- coeffs_out: float32 [96, 1024, 1000], P('row', 'col')
All inputs are finite; a program needn't handle non-finite values.
Results may differ from a plain program's by a relative error of at most 0.0003.
Values may be sent and summed in bfloat16 or wider, within the bound.
A program may use at most 64 MiB of HBM per device.

v0:
```python
import jax
import jax.numpy as jnp
from jax import lax
from jax.sharding import PartitionSpec as P

STEPS = 2
ridge_weight = 1.0


def broadcast(value, axis, source):
    kept = jnp.where(lax.axis_index(axis) == source, value, 0).astype(value.dtype)
    return lax.psum(kept, axis)


def on_device(points, targets, coeffs, block_inverse, block_order):
    blocks_here, per_col, features = points.shape
    classes = targets.shape[2]
    my_row = lax.axis_index("row")
    my_col = lax.axis_index("col")
    flat_points = points.reshape(blocks_here * per_col, features)
    flat_wide = flat_points.astype(jnp.float32)
    point_squares = jnp.sum(flat_wide * flat_wide, axis=1)
    current = coeffs
    for sweep_step in range(STEPS):
        block_id = block_order[sweep_step]
        local_index = block_id % blocks_here
        owner_row = block_id // blocks_here
        own_slice = lax.dynamic_index_in_dim(points, local_index, 0, keepdims=False)
        full_block = lax.all_gather(own_slice, "col", axis=0, tiled=True)
        active = broadcast(full_block, "row", owner_row)
        active_wide = active.astype(jnp.float32)
        active_squares = jnp.sum(active_wide * active_wide, axis=1)
        inner = lax.dot_general(
            active, flat_points, (((1,), (1,)), ((), ())), preferred_element_type=jnp.float32
        )
        distance = active_squares[:, None] + point_squares[None, :] - 2.0 * inner
        tile_wide = jnp.exp(-distance * (0.5 / features))
        flat_current = current.reshape(blocks_here * per_col, classes)
        products = jnp.dot(
            tile_wide,
            flat_current,
            precision=lax.Precision.HIGHEST,
            preferred_element_type=jnp.float32,
        )
        summed = lax.psum(products, ("row", "col"))
        own_sum = lax.dynamic_slice_in_dim(summed, my_col * per_col, per_col, 0)
        previous = lax.dynamic_index_in_dim(current, local_index, 0, keepdims=False)
        wanted = lax.dynamic_index_in_dim(targets, local_index, 0, keepdims=False).astype(
            jnp.float32
        )
        residual = wanted - own_sum - ridge_weight * previous
        full_residual = lax.all_gather(residual, "col", axis=0, tiled=True)
        inverse_rows = lax.dynamic_index_in_dim(block_inverse, local_index, 0, keepdims=False)
        increment = jnp.dot(
            inverse_rows,
            full_residual,
            precision=lax.Precision.HIGHEST,
            preferred_element_type=jnp.float32,
        )
        updated = jnp.where(my_row == owner_row, previous + increment, previous)
        current = lax.dynamic_update_index_in_dim(current, updated, local_index, 0)
    return current


def solution(mesh):
    placed = (
        P("row", "col", None),
        P("row", "col", None),
        P("row", "col", None),
        P("row", "col", None),
        P(),
    )
    return jax.shard_map(
        on_device, mesh=mesh, in_specs=placed, out_specs=P("row", "col", None), check_vma=False
    )
```

profile of v0, /device:TPU:1, one launch (start us, length us, event | category | flops | bytes accessed | tf_op | source)
XLA Modules:
  0.0 974.1 jit_solution(10416053570746938592)
XLA Ops:
  6.5 0.0 copy-start
  6.5 0.0 copy-start.5
  6.5 0.0 all-gather.13.cloned.1.call-start
  6.5 1.5 copy.13
  8.1 0.0 copy-done.5
  8.1 0.6 fusion.40
  9.8 1.7 constant_dynamic-slice_fusion.2
  11.5 0.0 all-gather.13.cloned.1.call-update
  11.5 0.0 all-gather.11.cloned.1.call-start
  11.6 0.7 all-gather.11.cloned.1.call-update
  12.3 0.0 all-reduce.9.cloned.1.call-start
  14.6 53.9 %all-gather.13.cloned.1.call-done = bf16[1,1024,1024]{2,1,0:T(8,128)(2,1)} async-done(((bf16[1,64,1024]{2,1,0:T(8,128)(2,1)}), bf16[1,1024,1024]{2,1,0:T(8,128)(2,1)}) %all-gather.13.cloned.1.call-update) | async-done | bytes 2097168 | tf_op jit(solution)/shard_map/all_gather | solution.py:29
  68.5 1.5 select_bitcast_fusion
  69.9 52.7 %all-gather.11.cloned.1.call-done = bf16[1,1024,1024]{2,1,0:T(8,128)(2,1)} async-done(((bf16[1,64,1024]{2,1,0:T(8,128)(2,1)}), bf16[1,1024,1024]{2,1,0:T(8,128)(2,1)}) %all-gather.11.cloned.1.call-update) | async-done | bytes 2097168 | tf_op jit(solution)/shard_map/all_gather | solution.py:29
  122.7 1.4 select_bitcast_fusion.1
  124.1 0.0 all-reduce.9.cloned.1.call-update
  124.1 0.0 all-reduce.5.cloned.1.call-start
  124.2 1.4 multiply_reduce_fusion.2
  125.6 0.1 add.75
  125.6 143.2 %all-reduce.9.cloned.1.call-done = (bf16[1024,1024]{1,0:T(8,128)(2,1)}, bf16[1024,1024]{1,0:T(8,128)(2,1)}) async-done(((bf16[1024,1024]{1,0:T(8,128)(2,1)}, bf16[1024,1024]{1,0:T(8,128)(2,1)}), (bf16[1024,1024]{1,0:T(8,128)(2,1)}, bf16[1024,1024]{1,0:T(8,128)(2,1)})) %all-reduce.9.cloned.1.call-update) | async-done | bytes 4194320 | tf_op jit(solution)/shard_map/psum | solution.py:12
  268.9 2.2 multiply_reduce_fusion.1
  271.1 0.0 copy-done.3
  271.1 2.4 fusion.41
  273.5 8.6 fusion.7
  282.1 0.0 all-reduce.5.cloned.1.call-update
  282.1 0.0 all-gather.7.cloned.1.call-start
  282.2 273.4 %all-reduce.5.cloned.1.call-done = f32[1024,1000]{1,0:T(8,128)} async-done(((f32[1024,1000]{1,0:T(8,128)}), f32[1024,1000]{1,0:T(8,128)}) %all-reduce.5.cloned.1.call-update) | async-done | bytes 4096016 | tf_op jit(solution)/shard_map/psum | solution.py:45
  555.6 1.7 fusion.29
  557.3 0.0 all-gather.7.cloned.1.call-update
  557.3 0.2 all-reduce.7.cloned.1.call-start
  557.5 0.0 copy-start.2
  557.6 2.2 multiply_reduce_fusion
  559.8 0.0 copy-done.2
  559.8 3.6 fusion.42
  563.4 56.2 %all-gather.7.cloned.1.call-done = f32[1024,1000]{1,0:T(8,128)} async-done(((f32[64,1000]{1,0:T(8,128)}), f32[1024,1000]{1,0:T(8,128)}) %all-gather.7.cloned.1.call-update) | async-done | bytes 4096016 | tf_op jit(solution)/shard_map/all_gather | solution.py:52
  619.6 0.0 copy-done
  619.6 4.9 fusion.19
  624.6 0.0 copy-start.1
  624.6 0.0 copy-done.4
  624.6 8.6 fusion
  633.2 0.0 all-reduce.7.cloned.1.call-update
  633.2 0.0 all-gather.9.cloned.1.call-start
  633.3 264.6 %all-reduce.7.cloned.1.call-done = f32[1024,1000]{1,0:T(8,128)} async-done(((f32[1024,1000]{1,0:T(8,128)}), f32[1024,1000]{1,0:T(8,128)}) %all-reduce.7.cloned.1.call-update) | async-done | bytes 4096016 | tf_op jit(solution)/shard_map/psum | solution.py:45
  897.9 1.7 fusion.28
  899.6 0.0 all-gather.9.cloned.1.call-update
  899.6 0.0 copy-done.1
  899.6 62.0 %all-gather.9.cloned.1.call-done = f32[1024,1000]{1,0:T(8,128)} async-done(((f32[64,1000]{1,0:T(8,128)}), f32[1024,1000]{1,0:T(8,128)}) %all-gather.9.cloned.1.call-update) | async-done | bytes 4096016 | tf_op jit(solution)/shard_map/all_gather | solution.py:52
  961.7 5.5 fusion.16
  (4 shorter events, 0.1 us)
Async XLA Ops:
  6.5 613.1 %copy-start = (f32[6,64,1024]{2,1,0:T(8,128)S(1)}, f32[6,64,1024]{2,1,0:T(8,128)}, u32[]{:S(2)}) copy-start(f32[6,64,1024]{2,1,0:T(8,128)} %param.8) | copy-start | bytes 4718596
  6.5 1.5 copy-start.5
  6.5 61.9 %all-gather.13.cloned.1.call-start = ((), (), s32[]{:S(2)}) async-start(), calls=%async_computation.5 | async-start | bytes 2228224 | tf_op jit(solution)/shard_map/all_gather | solution.py:29
  11.5 111.2 %all-gather.11.cloned.1.call-start = ((), (), s32[]{:S(2)}) async-start(), calls=%async_computation.4 | async-start | bytes 2228224 | tf_op jit(solution)/shard_map/all_gather | solution.py:29
  12.3 256.6 %all-reduce.9.cloned.1.call-start = ((), (), s32[]{:S(2)}) async-start(), calls=%async_computation.6 | async-start | bytes 8388608 | tf_op jit(solution)/shard_map/psum | solution.py:12
  124.1 431.4 %all-reduce.5.cloned.1.call-start = ((), (), s32[]{:S(2)}) async-start(), calls=%async_computation | async-start | bytes 8388608 | tf_op jit(solution)/shard_map/psum | solution.py:45
  268.9 2.2 copy-start.3
  282.1 337.5 %all-gather.7.cloned.1.call-start = ((), (), s32[]{:S(2)}) async-start(), calls=%async_computation.1 | async-start | bytes 4456448 | tf_op jit(solution)/shard_map/all_gather | solution.py:52
  557.3 340.5 %all-reduce.7.cloned.1.call-start = ((), (), s32[]{:S(2)}) async-start(), calls=%async_computation.2 | async-start | bytes 8388608 | tf_op jit(solution)/shard_map/psum | solution.py:45
  557.5 2.3 copy-start.2
  619.6 5.0 copy-start.4
  624.6 275.0 %copy-start.1 = (f32[6,64,1000]{2,1,0:T(8,128)}, f32[6,64,1000]{2,1,0:T(8,128)S(1)}, u32[]{:S(2)}) copy-start(f32[6,64,1000]{2,1,0:T(8,128)S(1)} %fusion.19) | copy-start | bytes 4608004
  633.2 328.5 %all-gather.9.cloned.1.call-start = ((), (), s32[]{:S(2)}) async-start(), calls=%async_computation.3 | async-start | bytes 4456448 | tf_op jit(solution)/shard_map/all_gather | solution.py:52
Sparse Core Ops, SparseCore 0:
  11.6 56.7 all-gather.12
  71.2 51.4 all-gather.10
  125.4 143.4 all-reduce.8
  282.3 273.2 all-reduce.4
  558.5 61.0 all-gather.6
  633.3 264.4 all-reduce.6
  900.6 61.0 all-gather.8
where the time goes:
time: 974 us
  waiting for transfers between devices  907 us (93%)
  matrix products  33.7 us (3%)
  between operations  17 us (2%)
  other arithmetic  12.2 us (1%)
    psum x2, waiting for transfers between devices, on_device(): summed = lax.psum(products, ('row', 'col'))  538 us
    psum x1, waiting for transfers between devices, broadcast(): return lax.psum(kept, axis)  143 us
    all_gather x2, waiting for transfers between devices, on_device(): full_residual = lax.all_gather(residual, 'col', axis=0, tiled=True)  118 us
    all_gather x2, waiting for transfers between devices, on_device(): full_block = lax.all_gather(own_slice, 'col', axis=0, tiled=True)  107 us
  transfers between devices with their start and end apart: 7, of which 7 were waited for; matrix products, arithmetic and copies ran while one was open for 1% of the time, Pallas kernels for 0%

commit v1 on v0

--- a/solution.py
+++ b/solution.py
@@ -42,7 +42,7 @@
             precision=lax.Precision.HIGHEST,
             preferred_element_type=jnp.float32,
         )
-        summed = lax.psum(products, ("row", "col"))
+        summed = lax.psum(lax.psum(products, "col"), "row")
         own_sum = lax.dynamic_slice_in_dim(summed, my_col * per_col, per_col, 0)
         previous = lax.dynamic_index_in_dim(current, local_index, 0, keepdims=False)
         wanted = lax.dynamic_index_in_dim(targets, local_index, 0, keepdims=False).astype(

time: 974 us -> 1060 us (1.088)
  waiting for transfers between devices: 907 us -> 992 us
    psum x2 -> x4, waiting for transfers between devices: 538 us -> 611 us  [on_device(): summed = lax.psum(lax.psum(products, 'col'), 'row')]
    all_gather x2, waiting for transfers between devices: 118 us -> 130 us  [on_device(): full_residual = lax.all_gather(residual, 'col', axis=0, tiled=True)]
  transfers between devices with their start and end apart: 7 -> 9, of which waited for: 7 -> 9; matrix products, arithmetic and copies ran while one was open for 1% -> 1% of each run, Pallas kernels for 0% -> 0%
where the time goes in v1:
time: 1060 us
  waiting for transfers between devices  992 us (94%)
  matrix products  33.7 us (3%)
  between operations  16.7 us (2%)
  other arithmetic  12.2 us (1%)
    psum x4, waiting for transfers between devices, on_device(): summed = lax.psum(lax.psum(products, 'col'), 'row')  611 us
    psum x1, waiting for transfers between devices, broadcast(): return lax.psum(kept, axis)  143 us
    all_gather x2, waiting for transfers between devices, on_device(): full_residual = lax.all_gather(residual, 'col', axis=0, tiled=True)  130 us
    all_gather x2, waiting for transfers between devices, on_device(): full_block = lax.all_gather(own_slice, 'col', axis=0, tiled=True)  107 us
  transfers between devices with their start and end apart: 9, of which 9 were waited for; matrix products, arithmetic and copies ran while one was open for 1% of the time, Pallas kernels for 0%

profile of v1, /device:TPU:1, one launch (start us, length us, event | category | flops | bytes accessed | tf_op | source)
XLA Modules:
  0.0 1058.9 jit_solution(2426635903485950652)
XLA Ops:
  6.5 0.0 copy-start
  6.5 0.0 all-gather.13.cloned.1.call-start
  6.5 1.5 copy.15
  8.1 0.0 copy-done.5
  8.1 0.6 fusion.40
  9.8 1.7 constant_dynamic-slice_fusion.2
  11.5 0.0 all-gather.13.cloned.1.call-update
  11.5 0.0 all-gather.11.cloned.1.call-start
  11.6 0.7 all-gather.11.cloned.1.call-update
  12.3 0.0 all-reduce.15.cloned.1.call-start
  14.6 53.9 %all-gather.13.cloned.1.call-done = bf16[1,1024,1024]{2,1,0:T(8,128)(2,1)} async-done(((bf16[1,64,1024]{2,1,0:T(8,128)(2,1)}), bf16[1,1024,1024]{2,1,0:T(8,128)(2,1)}) %all-gather.13.cloned.1.call-update) | async-done | bytes 2097168 | tf_op jit(solution)/shard_map/all_gather | solution.py:29
  68.5 1.5 select_bitcast_fusion
  69.9 52.7 %all-gather.11.cloned.1.call-done = bf16[1,1024,1024]{2,1,0:T(8,128)(2,1)} async-done(((bf16[1,64,1024]{2,1,0:T(8,128)(2,1)}), bf16[1,1024,1024]{2,1,0:T(8,128)(2,1)}) %all-gather.11.cloned.1.call-update) | async-done | bytes 2097168 | tf_op jit(solution)/shard_map/all_gather | solution.py:29
  122.7 1.4 select_bitcast_fusion.1
  124.1 0.0 all-reduce.15.cloned.1.call-update
  124.1 0.0 all-reduce.7.cloned.1.call-start
  124.2 1.4 multiply_reduce_fusion.2
  125.6 0.1 add.79
  125.6 143.2 %all-reduce.15.cloned.1.call-done = (bf16[1024,1024]{1,0:T(8,128)(2,1)}, bf16[1024,1024]{1,0:T(8,128)(2,1)}) async-done(((bf16[1024,1024]{1,0:T(8,128)(2,1)}, bf16[1024,1024]{1,0:T(8,128)(2,1)}), (bf16[1024,1024]{1,0:T(8,128)(2,1)}, bf16[1024,1024]{1,0:T(8,128)(2,1)})) %all-reduce.15.cloned.1.call-update) | async-done | bytes 4194320 | tf_op jit(solution)/shard_map/psum | solution.py:12
  268.9 2.2 multiply_reduce_fusion.1
  271.1 2.4 fusion.41
  273.5 8.6 fusion.7
  282.1 0.0 all-reduce.7.cloned.1.call-update
  282.1 0.0 all-reduce.9.cloned.1.call-start
  282.2 161.3 %all-reduce.7.cloned.1.call-done = f32[1024,1000]{1,0:T(8,128)} async-done(((f32[1024,1000]{1,0:T(8,128)}), f32[1024,1000]{1,0:T(8,128)}) %all-reduce.7.cloned.1.call-update) | async-done | bytes 4096016 | tf_op jit(solution)/shard_map/psum | solution.py:45
  443.4 0.0 all-reduce.9.cloned.1.call-update
  443.5 0.0 all-gather.7.cloned.1.call-start
  443.5 148.7 %all-reduce.9.cloned.1.call-done = f32[1024,1000]{1,0:T(8,128)} async-done(((f32[1024,1000]{1,0:T(8,128)}), f32[1024,1000]{1,0:T(8,128)}) %all-reduce.9.cloned.1.call-update) | async-done | bytes 4096016 | tf_op jit(solution)/shard_map/psum | solution.py:45
  592.2 1.7 fusion.29
  593.9 0.0 all-gather.7.cloned.1.call-update
  593.9 0.2 all-reduce.11.cloned.1.call-start
  594.2 2.2 multiply_reduce_fusion
  596.4 3.6 fusion.42
  600.0 61.9 %all-gather.7.cloned.1.call-done = f32[1024,1000]{1,0:T(8,128)} async-done(((f32[64,1000]{1,0:T(8,128)}), f32[1024,1000]{1,0:T(8,128)}) %all-gather.7.cloned.1.call-update) | async-done | bytes 4096016 | tf_op jit(solution)/shard_map/all_gather | solution.py:52
  661.9 4.9 fusion.19
  666.8 0.0 copy-start.1
  666.8 0.0 copy-done.4
  666.9 8.6 fusion
  675.5 0.0 all-reduce.11.cloned.1.call-update
  675.5 0.0 all-reduce.13.cloned.1.call-start
  675.5 152.5 %all-reduce.11.cloned.1.call-done = f32[1024,1000]{1,0:T(8,128)} async-done(((f32[1024,1000]{1,0:T(8,128)}), f32[1024,1000]{1,0:T(8,128)}) %all-reduce.11.cloned.1.call-update) | async-done | bytes 4096016 | tf_op jit(solution)/shard_map/psum | solution.py:45
  828.0 0.0 all-reduce.13.cloned.1.call-update
  828.0 0.0 all-gather.9.cloned.1.call-start
  828.1 149.0 %all-reduce.13.cloned.1.call-done = f32[1024,1000]{1,0:T(8,128)} async-done(((f32[1024,1000]{1,0:T(8,128)}), f32[1024,1000]{1,0:T(8,128)}) %all-reduce.13.cloned.1.call-update) | async-done | bytes 4096016 | tf_op jit(solution)/shard_map/psum | solution.py:45
  977.0 1.7 fusion.28
  978.8 0.0 all-gather.9.cloned.1.call-update
  978.9 68.0 %all-gather.9.cloned.1.call-done = f32[1024,1000]{1,0:T(8,128)} async-done(((f32[64,1000]{1,0:T(8,128)}), f32[1024,1000]{1,0:T(8,128)}) %all-gather.9.cloned.1.call-update) | async-done | bytes 4096016 | tf_op jit(solution)/shard_map/all_gather | solution.py:52
  1046.9 5.5 fusion.16
  (10 shorter events, 0.1 us)
Async XLA Ops:
  6.5 655.3 %copy-start = (f32[6,64,1024]{2,1,0:T(8,128)S(1)}, f32[6,64,1024]{2,1,0:T(8,128)}, u32[]{:S(2)}) copy-start(f32[6,64,1024]{2,1,0:T(8,128)} %param.8) | copy-start | bytes 4718596
  6.5 1.5 copy-start.5
  6.5 61.9 %all-gather.13.cloned.1.call-start = ((), (), s32[]{:S(2)}) async-start(), calls=%async_computation.7 | async-start | bytes 2228224 | tf_op jit(solution)/shard_map/all_gather | solution.py:29
  11.5 111.2 %all-gather.11.cloned.1.call-start = ((), (), s32[]{:S(2)}) async-start(), calls=%async_computation.6 | async-start | bytes 2228224 | tf_op jit(solution)/shard_map/all_gather | solution.py:29
  12.3 256.6 %all-reduce.15.cloned.1.call-start = ((), (), s32[]{:S(2)}) async-start(), calls=%async_computation.8 | async-start | bytes 8388608 | tf_op jit(solution)/shard_map/psum | solution.py:12
  124.1 319.3 %all-reduce.7.cloned.1.call-start = ((), (), s32[]{:S(2)}) async-start(), calls=%async_computation | async-start | bytes 8388608 | tf_op jit(solution)/shard_map/psum | solution.py:45
  268.9 2.2 copy-start.3
  282.1 310.1 %all-reduce.9.cloned.1.call-start = ((), (), s32[]{:S(2)}) async-start(), calls=%async_computation.1 | async-start | bytes 8388608 | tf_op jit(solution)/shard_map/psum | solution.py:45
  443.5 218.4 %all-gather.7.cloned.1.call-start = ((), (), s32[]{:S(2)}) async-start(), calls=%async_computation.2 | async-start | bytes 4456448 | tf_op jit(solution)/shard_map/all_gather | solution.py:52
  593.9 234.0 %all-reduce.11.cloned.1.call-start = ((), (), s32[]{:S(2)}) async-start(), calls=%async_computation.3 | async-start | bytes 8388608 | tf_op jit(solution)/shard_map/psum | solution.py:45
  594.2 2.3 copy-start.2
  661.9 5.0 copy-start.4
  666.8 312.0 %copy-start.1 = (f32[6,64,1000]{2,1,0:T(8,128)}, f32[6,64,1000]{2,1,0:T(8,128)S(1)}, u32[]{:S(2)}) copy-start(f32[6,64,1000]{2,1,0:T(8,128)S(1)} %fusion.19) | copy-start | bytes 4608004
  675.5 301.6 %all-reduce.13.cloned.1.call-start = ((), (), s32[]{:S(2)}) async-start(), calls=%async_computation.4 | async-start | bytes 8388608 | tf_op jit(solution)/shard_map/psum | solution.py:45
  828.0 218.9 %all-gather.9.cloned.1.call-start = ((), (), s32[]{:S(2)}) async-start(), calls=%async_computation.5 | async-start | bytes 4456448 | tf_op jit(solution)/shard_map/all_gather | solution.py:52
Sparse Core Ops, SparseCore 0:
  11.6 56.7 all-gather.12
  71.2 51.4 all-gather.10
  125.4 143.4 all-reduce.14
  282.3 161.1 all-reduce.6
  446.0 146.2 all-reduce.8
  594.8 67.0 all-gather.6
  675.6 152.3 all-reduce.10
  830.7 146.3 all-reduce.12
  979.8 67.0 all-gather.8
